TPU v7x, 256 devices: a whole 4x4x8 slice. The times are simulated.
256 devices in a mesh: branch: 2 (over x_lo), head: 4 (over y), tokens: 32 (over z, x_hi, core).
Axes of the slice: x: 4 (x_hi: 2, x_lo: 2; x = x_hi * 2 + x_lo), y: 4, z: 8, core: 2. Of those that a mesh axis runs over, the one named last changes fastest.
Arguments:
- queries: bfloat16 [2, 36864, 1536], P('branch', 'tokens', 'head'), may hold values from -128 to 128
- keys: bfloat16 [2, 36864, 1536], P('branch', 'tokens', 'head'), may hold values from -4 to 4
- values: bfloat16 [2, 36864, 1536], P('branch', 'tokens', 'head'), may hold values from -96 to 96
- residual: bfloat16 [2, 36864, 2, 1536], P('branch', 'tokens', None, 'head'), may hold values from -3 to 3
- gate: bfloat16 [2, 2, 1536], replicated, may hold values from 0.099609375 to 1.8984375
- out_weight: bfloat16 [1536, 3072], P('head'), may hold values from -0.15625 to 0.15625
- time_offsets: int32 [3, 32], replicated, may hold values from 0 to 1
- guidance_index: int32 [18], replicated, may hold values from 0 to 7
Outputs:
- guided: bfloat16 [36864, 3072], P('tokens', ('branch', 'head'))
All inputs are finite; a program needn't handle non-finite values.
Results may differ from a plain program's by a relative error of at most 0.0051.
Values may be sent and summed in bfloat16 or wider, within the bound.
A program may use at most 128 MiB of HBM per device.

v0:
```python
import math

import jax
import jax.numpy as jnp
from jax import lax
from jax.sharding import PartitionSpec as P

HD = 128
TT = 6
TH = 8
TW = 8


def with_halo(block, sides, width):
    for axis, dim in sides:
        count = lax.axis_size(axis)
        forward = [(i, i + 1) for i in range(count - 1)]
        backward = [(target, source) for source, target in forward]
        low = lax.ppermute(
            lax.slice_in_dim(block, block.shape[dim] - width, None, axis=dim), axis, forward
        )
        high = lax.ppermute(lax.slice_in_dim(block, 0, width, axis=dim), axis, backward)
        block = jnp.concatenate([low, block, high], axis=dim)
    return block


def partner_2(value, axis, bit):
    return lax.ppermute(value, axis, [(i, i ^ 1 << bit) for i in range(lax.axis_size(axis))])


def local(queries, keys, values, residual, gate, out_weight, time_offsets, guidance_index):
    tile_size = TT * TH * TW
    query_rows = queries[0]
    row_count = query_rows.shape[0]
    feature_count = query_rows.shape[1]
    tiles_time = time_offsets.shape[0]
    tiles_wide = time_offsets.shape[1]
    column = tiles_time * tile_size
    local_width = row_count // column
    width_pos = lax.axis_index("tokens")
    key_value = jnp.stack([keys[0], values[0]])
    region = with_halo(key_value, (("tokens", 1),), column)
    near_steps = jnp.arange(3, dtype=jnp.int32) - 1
    time_range = jnp.arange(tiles_time, dtype=jnp.int32)
    width_grid = jnp.arange(tiles_wide, dtype=jnp.int32)
    score_scale = 1.0 / math.sqrt(HD)
    heads_dev = feature_count // HD
    width_query = width_pos * local_width + 0
    width_key = width_query + near_steps
    width_ok = (width_key >= 0) & (width_key < tiles_wide)
    offset = jnp.sum(jnp.where(width_grid[None, :] == width_query, time_offsets, 0), axis=1)
    lower = time_range[:, None] - offset[:, None]
    time_ok = (time_range[None, :] >= lower) & (time_range[None, :] <= lower + 1)
    allowed = width_ok[None, :, None, None] & time_ok[:, None, :, None]
    allowed = jnp.broadcast_to(allowed, (tiles_time, 3, tiles_time, tile_size)).reshape(
        tiles_time, 1, 3 * column
    )
    key_rows = region[0, 0 : 3 * column]
    value_rows = region[1, 0 : 3 * column]
    head_pieces = []
    for head_index in range(heads_dev):
        first = head_index * HD
        scores = (
            lax.dot_general(
                query_rows[:, first : first + HD],
                key_rows[:, first : first + HD],
                (((1,), (1,)), ((), ())),
                preferred_element_type=jnp.float32,
            )
            * score_scale
        )
        scores = scores.reshape(tiles_time, tile_size, 3 * column)
        masked = jnp.where(allowed, scores, -1e30)
        row_max = jnp.max(masked, axis=2, keepdims=True)
        weights = jnp.where(allowed, jnp.exp(masked - row_max), 0.0)
        norm_total = jnp.sum(weights, axis=2, keepdims=True)
        blended = jnp.einsum(
            "aqk,kd->aqd",
            weights.astype(jnp.bfloat16),
            value_rows[:, first : first + HD],
            preferred_element_type=jnp.float32,
        )
        head_pieces.append((blended / norm_total).reshape(column, HD).astype(jnp.bfloat16))
    pieces = jnp.concatenate(head_pieces, axis=1)
    head_count = lax.axis_size("head")
    head_pos = lax.axis_index("head")
    branch_pos = lax.axis_index("branch")
    half_full = gate.shape[2]
    half_width = half_full // head_count
    is_cond = branch_pos == 0
    guide_scale = 1.0 + 0.5 * guidance_index.astype(jnp.float32)
    token_scale = jnp.broadcast_to(
        guide_scale[None, :, None], (local_width, guidance_index.shape[0], TH * TW)
    ).reshape(row_count)
    weight_order = out_weight.reshape(out_weight.shape[0], 2, head_count, half_width)
    weight_order = jnp.transpose(weight_order, (0, 2, 1, 3)).reshape(
        out_weight.shape[0], 2 * head_count * half_width
    )
    own_share = lax.psum_scatter(
        lax.dot_general(
            weight_order, pieces, (((0,), (1,)), ((), ())), preferred_element_type=jnp.float32
        ),
        "head",
        scatter_dimension=0,
        tiled=True,
    )
    projected = own_share.T.reshape(row_count, 2, half_width)
    gate_mine = lax.dynamic_index_in_dim(gate, branch_pos, 0, keepdims=False)
    gate_block = lax.dynamic_slice_in_dim(gate_mine, head_pos * half_width, half_width, 1).astype(
        jnp.float32
    )
    hidden = residual[0].astype(jnp.float32) + gate_block[None, :, :] * projected
    mine = jnp.where(is_cond, hidden[:, 0], hidden[:, 1])
    outgoing = jnp.where(is_cond, hidden[:, 1], hidden[:, 0])
    partner = partner_2(outgoing, "branch", 0)
    conditional = jnp.where(is_cond, mine, partner)
    unconditional = jnp.where(is_cond, partner, mine)
    guided = unconditional + token_scale[:, None] * (conditional - unconditional)
    return guided.astype(jnp.bfloat16)


def solution(mesh):
    return jax.shard_map(
        local,
        mesh=mesh,
        in_specs=(
            P("branch", "tokens", "head"),
            P("branch", "tokens", "head"),
            P("branch", "tokens", "head"),
            P("branch", "tokens", None, "head"),
            P(),
            P("head", None),
            P(),
            P(),
        ),
        out_specs=P("tokens", ("branch", "head")),
        check_vma=False,
    )
```

profile of v0, /device:TPU:129, one launch (start us, length us, event | category | flops | bytes accessed | tf_op | source)
XLA Modules:
  0.0 321.4 jit_solution(9674466022181666681)
XLA Ops:
  6.5 0.0 reduce-scatter.2.cloned.1.call-start
  6.5 2.2 constant_dynamic-update-slice_fusion.1
  8.7 2.2 constant_dynamic-update-slice_fusion
  10.9 5.2 %collective-permute-start = (bf16[2,1152,384]{2,1,0:T(8,128)(2,1)}, bf16[2,1152,384]{2,1,0:T(8,128)(2,1)}, u32[]{:S(2)}, u32[]{:S(2)}) collective-permute-start(bf16[2,1152,384]{2,1,0:T(8,128)(2,1)} %constant_dynamic-update-slice_fusion), channel_id=1, source_target_pairs={{0,1},{1,2},{2,3},{3,4},{4,5},{5,6},{6,7},{7,8},{8,9},{9,10},{10,1... | collective-permute-start | bytes 5308424 | tf_op jit(solution)/shard_map/ppermute | solution.py:19
  16.1 1.9 collective-permute-start.1
  18.1 0.8 select_reduce_fusion
  18.9 0.1 fusion.34
  19.0 0.1 broadcast_and_fusion
  19.0 0.1 broadcast_in_dim.83
  19.2 3.0 copy.14
  22.2 1.6 copy.15
  23.8 31.0 %collective-permute-done = bf16[2,1152,384]{2,1,0:T(8,128)(2,1)} collective-permute-done((bf16[2,1152,384]{2,1,0:T(8,128)(2,1)}, bf16[2,1152,384]{2,1,0:T(8,128)(2,1)}, u32[]{:S(2)}, u32[]{:S(2)}) %collective-permute-start) | collective-permute-done | bytes 1769504 | tf_op jit(solution)/shard_map/ppermute | solution.py:19
  54.8 2.8 collective-permute-done.1
  57.6 3.5 %pad_maximum_fusion = bf16[2,3456,384]{2,1,0:T(8,128)(2,1)S(1)} fusion(bf16[2,1152,384]{2,1,0:T(8,128)(2,1)} %collective-permute-done.1, bf16[2,1152,384]{2,1,0:T(8,128)(2,1)} %constant_dynamic-update-slice_fusion, bf16[2,1152,384]{2,1,0:T(8,128)(2,1)} %collective-permute-done), kind=kLoop, calls=%fused_computation.25 | loop fusion | flops 15925248 | bytes 10616832 | tf_op jit(solution)/shard_map/concatenate | solution.py:23
  61.1 0.0 copy-start.3
  61.2 2.0 slice_bitcast_fusion
  63.2 0.0 copy-done.3
  63.2 2.2 convolution_multiply_fusion
  65.4 0.0 copy-start
  65.4 10.6 %fusion.3 = (f32[1152]{0:T(1024)}, f32[1152]{0:T(1024)}, f32[3456,1152]{0,1:T(8,128)}) fusion(pred[3,3456]{1,0:T(4,128)(4,1)S(1)} %broadcast_in_dim.84, f32[3456,1152]{0,1:T(8,128)S(1)} %convolution_multiply_fusion, bf16[1152,384]{1,0:T(8,128)(2,1)S(1)} %bitcast.109, bf16[3456,384]{1,0:T(8,128)(2,1)S(1)} %get-tuple-element.11), kind=kOutput, calls=%fused_computation.15 | convolution fusion | flops 1039120128 | bytes 33053184 | tf_op jit(solution)/shard_map/dot_general | solution.py:64
  76.0 0.0 copy-done
  76.0 1.3 sub.64
  77.3 1.3 sub.74
  78.6 21.3 %fusion = (f32[1152]{0:T(1024)}, f32[1152]{0:T(1024)}, f32[1152]{0:T(1024)}, f32[3456,1152]{0,1:T(8,128)}) fusion(f32[3456,1152]{0,1:T(8,128)} %get-tuple-element.14, f32[1152]{0:T(1024)} %get-tuple-element.8, pred[3,3456]{1,0:T(4,128)(4,1)S(1)} %broadcast_in_dim.84, f32[1152]{0:T(1024)} %get-tuple-element.9, f32[3456,1152]{0,1:T(8,128)} %copy-done, ...), kind=kOutput, calls=%fused_computation.9 | convolution fusion | flops 1063006848 | bytes 48992256 | tf_op jit(solution)/shard_map/dot_general | solution.py:64
  99.9 0.7 div.30
  100.6 0.7 sub.69
  101.4 0.0 copy-start.4
  101.4 0.0 copy-start.2
  101.4 0.0 copy-start.6
  101.4 9.5 %fusion.1 = f32[1152]{0:T(1024)S(1)} fusion(f32[3456,1152]{0,1:T(8,128)} %get-tuple-element.15, f32[1152]{0:T(1024)} %get-tuple-element.6, pred[3,3456]{1,0:T(4,128)(4,1)S(1)} %broadcast_in_dim.84), kind=kLoop, calls=%fused_computation.10 | loop fusion | flops 15924096 | bytes 15944832 | tf_op jit(solution)/shard_map/reduce_sum | solution.py:76
  110.9 0.0 copy-done.4
  110.9 0.0 copy-done.2
  111.0 0.0 copy-done.6
  111.0 0.0 slice-start
  111.0 0.0 slice-start.1
  111.0 8.3 %fusion.22 = bf16[3,384,128]{2,1,0:T(8,128)(2,1)S(1)} fusion(f32[3,384,3456]{2,1,0:T(8,128)} %bitcast.103, f32[3,384]{1,0:T(4,128)S(1)} %copy-done.6, pred[3,3456]{1,0:T(4,128)(4,1)S(1)} %broadcast_in_dim.84, bf16[3456,384]{1,0:T(8,128)(2,1)S(1)} %copy-done.2, f32[3,384]{1,0:T(4,128)S(1)} %div.30), kind=kOutput, calls=%fused_computation.42 | convolution fusion | flops 1035436032 | bytes 17131008 | tf_op jit(solution)/shard_map/aqk,kd->aqd/dot_general | solution.py:77
  119.3 0.0 slice-start.2
  119.3 0.0 slice-start.3
  119.4 0.0 copy-start.5
  119.4 8.3 %fusion.20 = bf16[3,384,128]{2,1,0:T(8,128)(2,1)S(1)} fusion(f32[3,384,3456]{2,1,0:T(8,128)} %bitcast.104, f32[3,384]{1,0:T(4,128)S(1)} %sub.69, pred[3,3456]{1,0:T(4,128)(4,1)S(1)} %broadcast_in_dim.84, bf16[3456,384]{1,0:T(8,128)(2,1)S(1)} %copy-done.2, f32[3,384]{1,0:T(4,128)S(1)} %div.33), kind=kOutput, calls=%fused_computation.40 | convolution fusion | flops 1035436032 | bytes 17131008 | tf_op jit(solution)/shard_map/aqk,kd->aqd/dot_general | solution.py:77
  127.7 0.0 slice-done
  127.7 0.0 slice-done.1
  127.7 0.0 slice-done.2
  127.8 0.0 slice-done.3
  127.8 0.0 copy-done.5
  127.8 0.0 copy-start.1
  127.8 3.1 fusion.18
  130.9 0.0 copy-done.1
  130.9 7.2 %convolution_bitcast_fusion = f32[3072,1152]{0,1:T(8,128)} fusion(bf16[384,3072]{0,1:T(8,128)(2,1)S(1)} %bitcast.106, bf16[1152,128]{1,0:T(8,128)(2,1)S(1)} %bitcast.113, bf16[1152,128]{1,0:T(8,128)(2,1)S(1)} %bitcast.112, bf16[1152,128]{1,0:T(8,128)(2,1)S(1)} %bitcast.111), kind=kOutput, calls=%fused_computation.18 | convolution fusion | flops 2720563200 | bytes 17399808 | tf_op jit(solution)/shard_map/dot_general | solution.py:100
  138.1 0.0 reduce-scatter.2.cloned.1.call-update
  138.1 0.0 copy-start.7
  138.1 0.8 bitcast_convert_fusion
  138.9 128.7 %reduce-scatter.2.cloned.1.call-done = f32[768,1152]{0,1:T(8,128)} async-done(((f32[3072,1152]{0,1:T(8,128)}), f32[768,1152]{0,1:T(8,128)}) %reduce-scatter.2.cloned.1.call-update) | async-done | bytes 3538960 | tf_op jit(solution)/shard_map/reduce_scatter | solution.py:99
  267.6 2.9 fusion.12
  270.5 1.4 select_bitcast_fusion
  271.9 1.2 collective-permute-start.2
  273.1 0.0 copy-done.7
  273.1 0.1 broadcast_in_dim.91
  273.1 0.7 broadcast_in_dim.92
  273.8 37.9 %collective-permute-done.2 = f32[1152,384]{1,0:T(8,128)} collective-permute-done((f32[1152,384]{1,0:T(8,128)}, f32[1152,384]{1,0:T(8,128)}, u32[]{:S(2)}, u32[]{:S(2)}) %collective-permute-start.2) | collective-permute-done | bytes 1769504 | tf_op jit(solution)/shard_map/ppermute | solution.py:28
  311.8 2.8 fusion.16
  (8 shorter events, 0.1 us)
Async XLA Ops:
  6.5 261.1 %reduce-scatter.2.cloned.1.call-start = ((), (), s32[]{:S(2)}) async-start(), calls=%async_computation.1 | async-start | bytes 17694720 | tf_op jit(solution)/shard_map/reduce_scatter | solution.py:99
  10.9 43.9 %collective-permute-start = (bf16[2,1152,384]{2,1,0:T(8,128)(2,1)}, bf16[2,1152,384]{2,1,0:T(8,128)(2,1)}, u32[]{:S(2)}, u32[]{:S(2)}) collective-permute-start(bf16[2,1152,384]{2,1,0:T(8,128)(2,1)} %constant_dynamic-update-slice_fusion), channel_id=1, source_target_pairs={{0,1},{1,2},{2,3},{3,4},{4,5},{5,6},{6,7},{7,8},{8,9},{9,10},{10,1... | collective-permute-start | bytes 5308424 | tf_op jit(solution)/shard_map/ppermute | solution.py:19
  16.1 41.5 %collective-permute-start.1 = (bf16[2,1152,384]{2,1,0:T(8,128)(2,1)}, bf16[2,1152,384]{2,1,0:T(8,128)(2,1)}, u32[]{:S(2)}, u32[]{:S(2)}) collective-permute-start(bf16[2,1152,384]{2,1,0:T(8,128)(2,1)} %constant_dynamic-update-slice_fusion), channel_id=1, source_target_pairs={{1,0},{2,1},{3,2},{4,3},{5,4},{6,5},{7,6},{8,7},{9,8},{10,9},{11,1... | collective-permute-start | bytes 5308424 | tf_op jit(solution)/shard_map/ppermute | solution.py:22
  61.1 2.0 copy-start.3
  65.4 10.6 %copy-start = (f32[3456,1152]{0,1:T(8,128)}, f32[3456,1152]{0,1:T(8,128)S(1)}, u32[]{:S(2)}) copy-start(f32[3456,1152]{0,1:T(8,128)S(1)} %convolution_multiply_fusion) | copy-start | bytes 47775748
  101.4 9.6 %copy-start.4 = (f32[1152]{0:T(1024)S(1)}, f32[1152]{0:T(1024)}, u32[]{:S(2)}) copy-start(f32[1152]{0:T(1024)} %get-tuple-element.7) | copy-start | bytes 13828
  101.4 9.6 %copy-start.2 = (bf16[3456,384]{1,0:T(8,128)(2,1)S(1)}, bf16[3456,384]{1,0:T(8,128)(2,1)}, u32[]{:S(2)}) copy-start(bf16[3456,384]{1,0:T(8,128)(2,1)} %get-tuple-element.10) | copy-start | bytes 7962628
  101.4 9.6 %copy-start.6 = (f32[3,384]{1,0:T(4,128)S(1)}, f32[3,384]{1,0:T(4,128)}, u32[]{:S(2)}) copy-start(f32[3,384]{1,0:T(4,128)} %sub.64) | copy-start | bytes 13828
  111.0 16.8 %slice-start = ((s8[15925248]{0:T(1024)(128)(4,1)}), s8[4194304]{0:T(1024)(128)(4,1)S(1)}, s32[]{:S(2)}) async-start(s8[15925248]{0:T(1024)(128)(4,1)} %bitcast.100), calls=%async_computation.2 | async-start | bytes 8388608
  111.0 16.8 %slice-start.1 = ((s8[15925248]{0:T(1024)(128)(4,1)}), s8[4194304]{0:T(1024)(128)(4,1)S(1)}, s32[]{:S(2)}) async-start(s8[15925248]{0:T(1024)(128)(4,1)} %bitcast.100), calls=%async_computation.3 | async-start | bytes 8388608
  119.3 8.4 %slice-start.2 = ((s8[15925248]{0:T(1024)(128)(4,1)}), s8[4194304]{0:T(1024)(128)(4,1)S(1)}, s32[]{:S(2)}) async-start(s8[15925248]{0:T(1024)(128)(4,1)} %bitcast.100), calls=%async_computation.4 | async-start | bytes 8388608
  119.3 8.4 %slice-start.3 = ((s8[15925248]{0:T(1024)(128)(4,1)}), s8[3342336]{0:T(1024)(128)(4,1)S(1)}, s32[]{:S(2)}) async-start(s8[15925248]{0:T(1024)(128)(4,1)} %bitcast.100), calls=%async_computation.5 | async-start | bytes 6684672
  119.4 8.4 %copy-start.5 = (f32[3,384]{1,0:T(4,128)S(1)}, f32[3,384]{1,0:T(4,128)}, u32[]{:S(2)}) copy-start(f32[3,384]{1,0:T(4,128)} %sub.74) | copy-start | bytes 13828
  127.8 3.1 copy-start.1
  138.1 135.0 %copy-start.7 = (s32[18]{0:T(128)S(1)}, s32[18]{0:T(128)}, u32[]{:S(2)}) copy-start(s32[18]{0:T(128)} %param.15) | copy-start | bytes 220
  271.9 39.9 %collective-permute-start.2 = (f32[1152,384]{1,0:T(8,128)}, f32[1152,384]{1,0:T(8,128)}, u32[]{:S(2)}, u32[]{:S(2)}) collective-permute-start(f32[1152,384]{1,0:T(8,128)} %select_bitcast_fusion), channel_id=1, source_target_pairs={{0,128},{128,0},{1,129},{129,1},{2,130},{130,2},{3,131},{131,3},{4... | collective-permute-start | bytes 5308424 | tf_op jit(solution)/shard_map/ppermute | solution.py:28
Sparse Core Ops, SparseCore 0:
  138.2 129.3 reduce-scatter.1
where the time goes:
time: 324 us; the launch traced here: 321 us
  waiting for transfers between devices  200 us (62%)
  matrix products  61.1 us (19%)
  other arithmetic  21.9 us (7%)
  local copies, waits for them, and re-layouts  15.9 us (5%)
  between operations  13.7 us (4%)
  starting transfers between devices  8.3 us (3%)
    reduce_scatter x1, waiting for transfers between devices, local(): lax.psum_scatter(lax.dot_general(weight_order, pieces, (((0,), (1,)), (()...  129 us
    ppermute x1, waiting for transfers between devices, partner_2(): lax.ppermute(value, axis, [(i, i ^ 1 << bit) for i in range(lax.axis_size...  37.9 us
    dot_general x3, matrix products, local(): lax.dot_general(query_rows[:, first:first + HD], key_rows[:, first:first...  34.2 us
    ppermute x1, waiting for transfers between devices, with_halo(): lax.ppermute(lax.slice_in_dim(block, block.shape[dim] - width, None, axis...  31 us
    dot_general x3, matrix products, local(): jnp.einsum('aqk,kd->aqd', weights.astype(jnp.bfloat16), value_rows[:, fir...  19.8 us
    reduce_sum x1, other arithmetic, local(): norm_total = jnp.sum(weights, axis=2, keepdims=True)  9.55 us
    dot_general x1, matrix products, local(): lax.dot_general(weight_order, pieces, (((0,), (1,)), ((), ())), preferred...  7.16 us
  transfers between devices with their start and end apart: 4, of which 4 were waited for; matrix products, arithmetic and copies ran while one was open for 2% of the time, Pallas kernels for 0%

commit v1 on v0

v1 whole, which is shorter than its diff:
```python
import math

import jax
import jax.numpy as jnp
from jax import lax
from jax.experimental import pallas as pl
from jax.experimental.pallas import tpu as pltpu
from jax.sharding import PartitionSpec as P

HD = 128
TILE = 384
FRAME = 64
BF = jnp.bfloat16
F32 = jnp.float32
SCALE = math.log2(math.e) / math.sqrt(HD)
WINDOW = 3
PIECES = 9


def kernel(
    offsets, guidance, gate, q_hbm, k_hbm, v_hbm, r_hbm, w_hbm, out_hbm,
    q_own, k_own, v_own, k_left, v_left, k_right, v_right, res, w_all, att, scores,
    own_half, x_send, x_recv, out_v,
    local_sem, halo_send, halo_recv, w_send, w_recv, a_send, a_recv, x_ssem, x_rsem, out_sem,
):
    branch = lax.axis_index("branch")
    head = lax.axis_index("head")
    width = lax.axis_index("tokens")
    widths = lax.axis_size("tokens")
    heads = lax.axis_size("head")
    features = q_own.shape[1]
    local_heads = features // HD
    tiles = q_own.shape[0] // TILE
    half_full = w_hbm.shape[1] // 2
    has_left = width > 0
    has_right = width < widths - 1
    peers = [lax.rem(head + d, heads) for d in range(1, heads)]

    def mine_columns(which, owner):
        half = branch if which == 0 else 1 - branch
        return pl.ds(pl.multiple_of(half * half_full + owner * features, HD), features)

    loads = [
        pltpu.make_async_copy(src, dst, local_sem.at[i])
        for i, (src, dst) in enumerate(
            ((k_hbm, k_own), (v_hbm, v_own), (q_hbm, q_own), (r_hbm, res))
        )
    ] + [
        pltpu.make_async_copy(
            w_hbm.at[:, mine_columns(which, head)],
            w_all.at[0, :, pl.ds(which * features, features)],
            local_sem.at[4 + which],
        )
        for which in range(2)
    ]
    for load in loads:
        load.start()

    barrier = pltpu.get_barrier_semaphore()

    @pl.when(has_left)
    def _():
        pl.semaphore_signal(barrier, inc=1, device_id={"tokens": width - 1})

    @pl.when(has_right)
    def _():
        pl.semaphore_signal(barrier, inc=1, device_id={"tokens": width + 1})

    for peer in peers:
        pl.semaphore_signal(barrier, inc=1, device_id={"head": peer})
    pl.semaphore_signal(barrier, inc=1, device_id={"branch": 1 - branch})
    pl.semaphore_wait(
        barrier, heads + has_left.astype(jnp.int32) + has_right.astype(jnp.int32)
    )

    def piece(index):
        early = index < 2 * local_heads
        tile = jnp.where(early, lax.rem(index, 2), 2)
        own_head = jnp.where(early, index // 2, index - 2 * local_heads)
        return (
            pl.ds(pl.multiple_of(tile * TILE, TILE), TILE),
            pl.ds(pl.multiple_of(own_head * HD, HD), HD),
        )

    def halo_copies(index, leftwards):
        where = piece(index)
        target = width - 1 if leftwards else width + 1
        place = 0 if leftwards else 2
        dests = (k_right, v_right) if leftwards else (k_left, v_left)
        return [
            pltpu.make_async_remote_copy(
                src_ref=src.at[where],
                dst_ref=dst.at[where],
                send_sem=halo_send.at[index, place + i],
                recv_sem=halo_recv.at[index, place + i],
                device_id={"tokens": target},
            )
            for i, (src, dst) in enumerate(zip((k_hbm, v_hbm), dests))
        ]

    def send_piece(index):
        @pl.when(has_left)
        def _():
            for copy in halo_copies(index, True):
                copy.start()

        @pl.when(has_right)
        def _():
            for copy in halo_copies(index, False):
                copy.start()

    def take_piece(index):
        @pl.when(has_right)
        def _():
            for copy in halo_copies(index, True):
                copy.wait_recv()

        @pl.when(has_left)
        def _():
            for copy in halo_copies(index, False):
                copy.wait_recv()

        @pl.when(index + WINDOW < PIECES)
        def _():
            send_piece(index + WINDOW)

    for index in range(WINDOW):
        send_piece(index)

    def w_copies(d):
        return [
            pltpu.make_async_remote_copy(
                src_ref=w_hbm.at[:, mine_columns(which, peers[d - 1])],
                dst_ref=w_all.at[heads - d, :, pl.ds(which * features, features)],
                send_sem=w_send.at[d - 1, which],
                recv_sem=w_recv.at[heads - d - 1, which],
                device_id={"head": peers[d - 1]},
            )
            for which in range(2)
        ]

    for d in range(1, heads):
        for copy in w_copies(d):
            copy.start()
    for load in loads:
        load.wait()

    @pl.when(jnp.logical_not(has_left))
    def _():
        k_left[...] = k_own[...]
        v_left[...] = jnp.zeros_like(v_left)

    @pl.when(jnp.logical_not(has_right))
    def _():
        k_right[...] = k_own[...]
        v_right[...] = jnp.zeros_like(v_right)

    columns = (
        (k_own, v_own, jnp.float32(1)),
        (k_left, v_left, has_left.astype(F32)),
        (k_right, v_right, has_right.astype(F32)),
    )

    def unit(tile, own_head):
        offset = offsets[tile, width]
        back = offset == 1
        second = jnp.where(back, tile - 1, tile + 1)
        valid = jnp.logical_and(second >= 0, second < tiles)
        rows = pl.ds(pl.multiple_of(tile * TILE, TILE), TILE)
        before = pl.ds(pl.multiple_of(jnp.maximum(tile - 1, 0) * TILE, TILE), TILE)
        after = pl.ds(pl.multiple_of(jnp.minimum(tile + 1, tiles - 1) * TILE, TILE), TILE)
        cols = pl.ds(pl.multiple_of(own_head * HD, HD), HD)
        query = q_own[rows, cols]
        top = None
        for i, (k_ref, _, _) in enumerate(columns):
            for which in range(2):
                if which == 0:
                    key = k_ref[rows, cols]
                else:
                    key = jnp.where(back, k_ref[before, cols], k_ref[after, cols])
                found = lax.dot_general(
                    query, key, (((1,), (1,)), ((), ())), preferred_element_type=F32
                )
                first = (2 * i + which) * TILE
                scores[:, first : first + TILE] = found
                for lane in range(0, TILE, HD):
                    part = found[:, lane : lane + HD]
                    top = part if top is None else jnp.maximum(top, part)
        top = jnp.max(top, axis=1, keepdims=True) * SCALE
        total = None
        for i, (_, v_ref, present) in enumerate(columns):
            for which in range(2):
                if which == 0:
                    value = v_ref[rows, cols]
                    count = present
                else:
                    value = jnp.where(back, v_ref[before, cols], v_ref[after, cols])
                    value = jnp.where(valid, value, jnp.zeros_like(value))
                    count = present * valid.astype(F32)
                ones = jnp.full((TILE, HD), count, F32).astype(BF)
                first = (2 * i + which) * TILE
                weights = jnp.exp2(scores[:, first : first + TILE] * SCALE - top).astype(BF)
                term = jnp.dot(
                    weights,
                    jnp.concatenate([value, ones], axis=1),
                    preferred_element_type=F32,
                )
                total = term if total is None else total + term
        att[0, rows, cols] = (total[:, :HD] / total[:, HD:]).astype(BF)

    def att_copies(tile, own_head):
        where = (
            pl.ds(pl.multiple_of(tile * TILE, TILE), TILE),
            pl.ds(pl.multiple_of(own_head * HD, HD), HD),
        )
        slot = tile * local_heads + own_head
        return [
            pltpu.make_async_remote_copy(
                src_ref=att.at[(0, *where)],
                dst_ref=att.at[(heads - d, *where)],
                send_sem=a_send.at[slot, d - 1],
                recv_sem=a_recv.at[slot, heads - d - 1],
                device_id={"head": peers[d - 1]},
            )
            for d in range(1, heads)
        ]

    def run_unit(tile, own_head):
        unit(tile, own_head)
        for copy in att_copies(tile, own_head):
            copy.start()

    @pl.loop(0, local_heads)
    def _(own_head):
        take_piece(2 * own_head)
        take_piece(2 * own_head + 1)
        run_unit(0, own_head)

    def exchange(tile):
        rows = pl.ds(tile * TILE, TILE)
        return pltpu.make_async_remote_copy(
            src_ref=x_send.at[rows],
            dst_ref=x_recv.at[rows],
            send_sem=x_ssem.at[tile],
            recv_sem=x_rsem.at[tile],
            device_id={"branch": 1 - branch},
        )

    gate_cols = pl.ds(pl.multiple_of(head * features, HD), features)

    def project(tile):
        rows = pl.ds(tile * TILE, TILE)
        for own_head in range(local_heads):
            for copy in att_copies(tile, own_head):
                copy.wait_recv()
        for which in (1, 0):
            half = branch if which == 0 else 1 - branch
            lanes = pl.ds(which * features, features)
            summed = None
            for slot in range(heads):
                term = jnp.dot(
                    att[slot, rows, :], w_all[slot, :, lanes], preferred_element_type=F32
                )
                summed = term if summed is None else summed + term
            scale = gate[pl.ds(branch * 2 + half, 1), gate_cols]
            hidden = res[half, rows, :].astype(F32) + scale * summed
            if which == 1:
                x_send[rows, :] = hidden.astype(BF)
                exchange(tile).start()
            else:
                own_half[rows, :] = hidden

    def combine(tile):
        exchange(tile).wait_recv()
        frames = TILE // FRAME
        for frame in range(frames):
            rows = pl.ds(tile * TILE + frame * FRAME, FRAME)
            step = guidance[tile * frames + frame].astype(F32)
            strength = 1.0 + 0.5 * step
            mine = jnp.where(branch == 0, strength, 1.0 - strength)
            theirs = 1.0 - mine
            guided = own_half[rows, :] * mine + x_recv[rows, :].astype(F32) * theirs
            out_v[rows, :] = guided.astype(BF)
        rows = pl.ds(tile * TILE, TILE)
        pltpu.make_async_copy(out_v.at[rows], out_hbm.at[rows], out_sem.at[tile]).start()

    for own_head in range(local_heads):
        take_piece(jnp.int32(2 * local_heads + own_head))

        @pl.loop(1, tiles)
        def _(tile):
            run_unit(tile, own_head)

        if own_head == 0:
            for d in range(1, heads):
                for copy in w_copies(d):
                    copy.wait_recv()
            project(0)

    for tile in range(1, tiles):
        project(tile)
    for tile in range(tiles):
        combine(tile)

    for tile in range(tiles):
        rows = pl.ds(tile * TILE, TILE)
        pltpu.make_async_copy(out_v.at[rows], out_hbm.at[rows], out_sem.at[tile]).wait()
        exchange(tile).wait_send()
    for d in range(1, heads):
        for copy in w_copies(d):
            copy.wait_send()

    @pl.loop(0, PIECES)
    def _(index):
        for copy in att_copies(index // local_heads, lax.rem(index, local_heads)):
            copy.wait_send()

        @pl.when(has_left)
        def _():
            for copy in halo_copies(index, True):
                copy.wait_send()

        @pl.when(has_right)
        def _():
            for copy in halo_copies(index, False):
                copy.wait_send()


def local(queries, keys, values, residual, gate, out_weight, time_offsets, guidance_index):
    rows, features = queries.shape[1:]
    heads = lax.axis_size("head")
    halves = jnp.transpose(residual[0], (1, 0, 2))
    gates = gate.reshape(4, gate.shape[2]).astype(F32)
    smem = pl.BlockSpec(memory_space=pltpu.SMEM)
    vmem = pl.BlockSpec(memory_space=pltpu.VMEM)
    hbm = pl.BlockSpec(memory_space=pl.ANY)
    block = pltpu.VMEM((rows, features), BF)
    dma = pltpu.SemaphoreType.DMA
    tiles = rows // TILE
    return pl.pallas_call(
        kernel,
        out_shape=jax.ShapeDtypeStruct((rows, features), BF),
        in_specs=[smem, smem, vmem, hbm, hbm, hbm, hbm, hbm],
        out_specs=hbm,
        scratch_shapes=[block] * 7
        + [
            pltpu.VMEM((2, rows, features), BF),
            pltpu.VMEM((heads, features, 2 * features), BF),
            pltpu.VMEM((heads, rows, features), BF),
            pltpu.VMEM((TILE, 6 * TILE), F32),
            pltpu.VMEM((rows, features), F32),
            block,
            block,
            block,
            dma((6,)),
            dma((PIECES, 4)),
            dma((PIECES, 4)),
            dma((heads - 1, 2)),
            dma((heads - 1, 2)),
            dma((PIECES, heads - 1)),
            dma((PIECES, heads - 1)),
            dma((tiles,)),
            dma((tiles,)),
            dma((tiles,)),
        ],
        compiler_params=pltpu.CompilerParams(
            collective_id=0, has_side_effects=True, vmem_limit_bytes=48 * 2**20
        ),
        name="block",
    )(time_offsets, guidance_index, gates, queries[0], keys[0], values[0], halves, out_weight)


def solution(mesh):
    return jax.shard_map(
        local,
        mesh=mesh,
        in_specs=(
            P("branch", "tokens", "head"),
            P("branch", "tokens", "head"),
            P("branch", "tokens", "head"),
            P("branch", "tokens", None, "head"),
            P(),
            P("head", None),
            P(),
            P(),
        ),
        out_specs=P("tokens", ("branch", "head")),
        check_vma=False,
    )
```

time: 324 us -> 89.8 us (0.28)
  the two profiles are of different devices: /device:TPU:129 before, /device:TPU:1 now
where the time goes in v1:
time: 89.8 us; the launch traced here: 89.6 us
  Pallas kernels  85.7 us (95%)
  local copies, waits for them, and re-layouts  3.83 us (4%)
    pallas_call x1, Pallas kernels, local(): pl.pallas_call(kernel, out_shape=jax.ShapeDtypeStruct((rows, features), B...  85.7 us
    unnamed x12, local copies, waits for them, and re-layouts  3.11 us

profile of v1, /device:TPU:1, one launch (start us, length us, event | category | flops | bytes accessed | tf_op | source)
XLA Modules:
  0.0 89.6 jit_solution(17949253890820942751)
XLA Ops:
  0.0 0.7 reshape.3.gate
  0.7 0.0 copy-start
  0.7 0.0 copy-start.1
  0.7 0.0 copy-start.2
  0.8 0.0 copy-start.3
  0.8 0.0 copy-start.4
  0.8 1.9 %copy.11 = bf16[1,1152,2,384]{3,1,2,0:T(8,128)(2,1)S(1)} copy(bf16[1,1152,2,384]{3,2,1,0:T(2,128)(2,1)} %param.11) | data formatting | bytes 3538944 | tf_op args[3]
  2.6 0.0 copy-done
  2.6 0.0 copy-done.1
  2.7 0.3 copy-done.2
  3.0 0.0 copy-done.3
  3.0 0.0 copy-done.4
  3.0 85.7 %block.1 = bf16[1152,384]{1,0:T(8,128)(2,1)S(1)} custom-call(s32[3,32]{1,0:T(4,128)S(1)} %copy-done.3, s32[18]{0:T(128)S(1)} %copy-done.4, f32[4,1536]{1,0:T(4,128)S(1)} %reshape.3.gate, bf16[1152,384]{1,0:T(8,128)(2,1)S(1)} %bitcast.9, bf16[1152,384]{1,0:T(8,128)(2,1)S(1)} %bitcast.10, bf16[1152,384]{1,0:T(8,128)(2,1)S(1)} %bitcast.11, ...), custom_call_target="tpu_custom_call" | custom-call | tf_op jit(solution)/shard_map/block/pallas_call | solution.py:340
  88.7 0.9 %copy.13 = bf16[1152,384]{1,0:T(8,128)(2,1)} copy(bf16[1152,384]{1,0:T(8,128)(2,1)S(1)} %block.1) | data formatting | bytes 1769472
Async XLA Ops:
  0.7 1.9 %copy-start = (bf16[1,1152,384]{2,1,0:T(8,128)(2,1)S(1)}, bf16[1,1152,384]{2,1,0:T(8,128)(2,1)}, u32[]{:S(2)}) copy-start(bf16[1,1152,384]{2,1,0:T(8,128)(2,1)} %param.8) | copy-start | bytes 2654212
  0.7 2.0 %copy-start.1 = (bf16[1,1152,384]{2,1,0:T(8,128)(2,1)S(1)}, bf16[1,1152,384]{2,1,0:T(8,128)(2,1)}, u32[]{:S(2)}) copy-start(bf16[1,1152,384]{2,1,0:T(8,128)(2,1)} %param.9) | copy-start | bytes 2654212
  0.7 2.2 %copy-start.2 = (bf16[1,1152,384]{2,1,0:T(8,128)(2,1)S(1)}, bf16[1,1152,384]{2,1,0:T(8,128)(2,1)}, u32[]{:S(2)}) copy-start(bf16[1,1152,384]{2,1,0:T(8,128)(2,1)} %param.10) | copy-start | bytes 2654212
  0.8 2.2 %copy-start.3 = (s32[3,32]{1,0:T(4,128)S(1)}, s32[3,32]{1,0:T(4,128)}, u32[]{:S(2)}) copy-start(s32[3,32]{1,0:T(4,128)} %offsets.1) | copy-start | bytes 1156
  0.8 2.2 %copy-start.4 = (s32[18]{0:T(128)S(1)}, s32[18]{0:T(128)}, u32[]{:S(2)}) copy-start(s32[18]{0:T(128)} %guidance.1) | copy-start | bytes 220

commit v2 on v1

v2 whole, which is shorter than its diff:
```python
import math

import jax
import jax.numpy as jnp
from jax import lax
from jax.experimental import pallas as pl
from jax.experimental.pallas import tpu as pltpu
from jax.sharding import PartitionSpec as P

HD = 128
TILE = 384
FRAME = 64
BF = jnp.bfloat16
F32 = jnp.float32
SCALE = math.log2(math.e) / math.sqrt(HD)
WINDOW = 3
PIECES = 9
VMEM = 62 * 2**20
PIECE_ORDER = ((0, 0), (1, 0), (2, 0), (0, 1), (1, 1), (0, 2), (1, 2), (2, 1), (2, 2))
UNIT_ORDER = ((0, 0), (1, 0), (2, 0), (0, 1), (0, 2), (1, 1), (2, 1), (1, 2), (2, 2))
NEEDED = (2, 3, 3, 5, 7, 8, 8, 9, 9)
BEGUN = (2, 3, 3, 6, 9, 9, 9, 9, 9)
DIRECT = (4, 7, 8)
LAG = 2
SHARE_AT = 2
PROJECT_AT = 6


def pick(index, table, field=None):
    found = 0
    for i, entry in enumerate(table):
        value = entry if field is None else entry[field]
        if value:
            found = found + jnp.where(index == i, value, 0)
    return found


def kernel(
    offsets, guidance, gate, q_hbm, k_hbm, v_hbm, r_hbm, w_hbm, out_hbm,
    q_own, k_own, v_own, k_near, v_near, k_far, v_far, res_raw, res, w_all, att, scores, tops, totals,
    own_half, x_send, x_recv, out_v,
    local_sem, near_send, near_recv, halo_send, halo_recv, w_send, w_recv, s_send, s_recv, a_send, a_recv, x_ssem, x_rsem, out_sem,
):
    branch = lax.axis_index("branch")
    head = lax.axis_index("head")
    width = lax.axis_index("tokens")
    widths = lax.axis_size("tokens")
    heads = lax.axis_size("head")
    features = q_own.shape[1]
    local_heads = features // HD
    tiles = q_own.shape[0] // TILE
    half_full = w_hbm.shape[1] // 2
    rows_all = q_own.shape[0]
    step = 1 - 2 * lax.rem(width, 2)
    sibling = width + step
    far = width - step
    has_far = jnp.logical_and(far >= 0, far < widths)
    peers = [lax.rem(head + d, heads) for d in range(1, heads)]

    def mine_columns(which, owner):
        half = branch if which == 0 else 1 - branch
        return pl.ds(pl.multiple_of(half * half_full + owner * features, HD), features)

    loads = [
        pltpu.make_async_copy(src, dst, local_sem.at[i])
        for i, (src, dst) in enumerate(
            ((k_hbm, k_own), (v_hbm, v_own), (q_hbm, q_own), (r_hbm, res_raw))
        )
    ] + [
        pltpu.make_async_copy(
            w_hbm.at[:, mine_columns(which, head)],
            w_all.at[0, :, pl.ds(which * features, features)],
            local_sem.at[4 + which],
        )
        for which in range(2)
    ]
    for load in loads:
        load.start()

    barrier = pltpu.get_barrier_semaphore()

    @pl.when(has_far)
    def _():
        pl.semaphore_signal(barrier, inc=1, device_id={"tokens": far})

    pl.semaphore_signal(barrier, inc=1, device_id={"tokens": sibling})
    for peer in peers:
        pl.semaphore_signal(barrier, inc=1, device_id={"head": peer})
    pl.semaphore_signal(barrier, inc=1, device_id={"branch": 1 - branch})
    pl.semaphore_wait(barrier, heads + 1 + has_far.astype(jnp.int32))

    near_copies = [
        pltpu.make_async_remote_copy(
            src_ref=src,
            dst_ref=dst,
            send_sem=near_send.at[i],
            recv_sem=near_recv.at[i],
            device_id={"tokens": sibling},
        )
        for i, (src, dst) in enumerate(((k_hbm, k_near), (v_hbm, v_near)))
    ]

    def piece(index):
        tile, own_head = pick(index, PIECE_ORDER, 0), pick(index, PIECE_ORDER, 1)
        return (
            pl.ds(pl.multiple_of(tile * TILE, TILE), TILE),
            pl.ds(pl.multiple_of(own_head * HD, HD), HD),
        )

    def far_copies(index):
        where = piece(index)
        return [
            pltpu.make_async_remote_copy(
                src_ref=src.at[where],
                dst_ref=dst.at[where],
                send_sem=halo_send.at[index, i],
                recv_sem=halo_recv.at[index, i],
                device_id={"tokens": far},
            )
            for i, (src, dst) in enumerate(((k_hbm, k_far), (v_hbm, v_far)))
        ]

    def send_piece(index):
        @pl.when(has_far)
        def _():
            for copy in far_copies(index):
                copy.start()

    def take_piece(index):
        @pl.when(has_far)
        def _():
            for copy in far_copies(index):
                copy.wait_recv()

        @pl.when(index + WINDOW < PIECES)
        def _():
            send_piece(index + WINDOW)

    for index in range(WINDOW):
        send_piece(index)

    share = features // 2
    mine = pl.ds(pl.multiple_of(lax.rem(width, 2) * share, share), share)
    others = pl.ds(pl.multiple_of((1 - lax.rem(width, 2)) * share, share), share)

    def w_copies(d):
        return [
            pltpu.make_async_remote_copy(
                src_ref=w_hbm.at[mine, mine_columns(which, peers[d - 1])],
                dst_ref=w_all.at[heads - d, mine, pl.ds(which * features, features)],
                send_sem=w_send.at[d - 1, which],
                recv_sem=w_recv.at[heads - d - 1, which],
                device_id={"head": peers[d - 1]},
            )
            for which in range(2)
        ]

    def w_share(slot, rows):
        return pltpu.make_async_remote_copy(
            src_ref=w_all.at[slot, rows],
            dst_ref=w_all.at[slot, rows],
            send_sem=s_send.at[slot - 1],
            recv_sem=s_recv.at[slot - 1],
            device_id={"tokens": sibling},
        )

    for d in range(1, heads):
        for copy in w_copies(d):
            copy.start()
    for copy in near_copies:
        copy.start()
    for load in loads:
        load.wait()
    for part in range(rows_all // FRAME):
        span = pl.ds(part * FRAME, FRAME)
        both = res_raw[span, :, :].astype(F32)
        for half in range(2):
            res[half, span, :] = both[:, half, :].astype(BF)

    @pl.when(jnp.logical_not(has_far))
    def _():
        k_far[...] = k_own[...]
        v_far[...] = jnp.zeros_like(v_far)

    early = ((k_own, v_own), (k_near, v_near))
    late = ((k_far, v_far),)

    def attend(tile, own_head, columns, present):
        offset = offsets[tile, width]
        back = offset == 1
        second = jnp.where(back, tile - 1, tile + 1)
        valid = jnp.logical_and(second >= 0, second < tiles)
        rows = pl.ds(pl.multiple_of(tile * TILE, TILE), TILE)
        before = pl.ds(pl.multiple_of(jnp.maximum(tile - 1, 0) * TILE, TILE), TILE)
        after = pl.ds(pl.multiple_of(jnp.minimum(tile + 1, tiles - 1) * TILE, TILE), TILE)
        cols = pl.ds(pl.multiple_of(own_head * HD, HD), HD)
        query = q_own[rows, cols]
        top = None
        for i, (k_ref, _) in enumerate(columns):
            for which in range(2):
                if which == 0:
                    key = k_ref[rows, cols]
                else:
                    key = jnp.where(back, k_ref[before, cols], k_ref[after, cols])
                found = lax.dot_general(
                    query, key, (((1,), (1,)), ((), ())), preferred_element_type=F32
                )
                first = (2 * i + which) * TILE
                scores[:, first : first + TILE] = found
                for lane in range(0, TILE, HD):
                    part = found[:, lane : lane + HD]
                    top = part if top is None else jnp.maximum(top, part)
        top = jnp.max(top, axis=1, keepdims=True) * SCALE

        def blend(top):
            total = None
            for i, (_, v_ref) in enumerate(columns):
                for which in range(2):
                    if which == 0:
                        value = v_ref[rows, cols]
                        count = present
                    else:
                        value = jnp.where(back, v_ref[before, cols], v_ref[after, cols])
                        value = jnp.where(valid, value, jnp.zeros_like(value))
                        count = present * valid.astype(F32)
                    ones = jnp.full((TILE, HD), count, F32).astype(BF)
                    first = (2 * i + which) * TILE
                    weights = jnp.exp2(scores[:, first : first + TILE] * SCALE - top).astype(BF)
                    term = jnp.dot(
                        weights,
                        jnp.concatenate([value, ones], axis=1),
                        preferred_element_type=F32,
                    )
                    total = term if total is None else total + term
            return total

        return top, blend

    def begin_unit(index):
        tile, own_head = pick(index, UNIT_ORDER, 0), pick(index, UNIT_ORDER, 1)
        top, blend = attend(tile, own_head, early, jnp.float32(1))
        tops[index] = jnp.broadcast_to(top, (TILE, HD))
        totals[index] = blend(top)

    def end_unit(tile, own_head, index):
        top, blend = attend(tile, own_head, late, has_far.astype(F32))
        old = tops[index][:, :1]
        new = jnp.maximum(old, top)
        total = blend(new) + totals[index] * jnp.exp2(old - new)
        rows = pl.ds(pl.multiple_of(tile * TILE, TILE), TILE)
        cols = pl.ds(pl.multiple_of(own_head * HD, HD), HD)
        att[0, rows, cols] = (total[:, :HD] / total[:, HD:]).astype(BF)

    def gather_copy(tile, own_head, kind):
        forwards = kind % 2 == 0
        own = kind != 2 and kind != 3
        first = tile * TILE + (0 if own or forwards else TILE // 2)
        count = TILE if own else TILE // 2
        where = (
            pl.ds(pl.multiple_of(first, TILE // 2), count),
            pl.ds(pl.multiple_of(own_head * HD, HD), HD),
        )
        came = heads - 1 if forwards else 1
        source = 0 if own else came
        dest = came if kind < 2 else 2
        target = peers[1] if kind == 4 else peers[0] if forwards else peers[-1]
        index = tile * local_heads + own_head
        return pltpu.make_async_remote_copy(
            src_ref=att.at[(source, *where)],
            dst_ref=att.at[(dest, *where)],
            send_sem=a_send.at[index, kind],
            recv_sem=a_recv.at[index, kind],
            device_id={"head": target},
        )

    def relay(tile, own_head):
        for kind in (0, 1):
            gather_copy(tile, own_head, kind).wait_recv()
            gather_copy(tile, own_head, kind + 2).start()

    def share_weights():
        for d in range(1, heads):
            for copy in w_copies(d):
                copy.wait_recv()
        for slot in range(1, heads):
            w_share(slot, mine).start()

    def exchange(tile):
        rows = pl.ds(tile * TILE, TILE)
        return pltpu.make_async_remote_copy(
            src_ref=x_send.at[rows],
            dst_ref=x_recv.at[rows],
            send_sem=x_ssem.at[tile],
            recv_sem=x_rsem.at[tile],
            device_id={"branch": 1 - branch},
        )

    gate_cols = pl.ds(pl.multiple_of(head * features, HD), features)

    def project(tile):
        rows = pl.ds(tile * TILE, TILE)
        for own_head in range(local_heads):
            direct = UNIT_ORDER.index((tile, own_head)) in DIRECT
            for kind in (0, 1, 4) if direct else (2, 3):
                gather_copy(tile, own_head, kind).wait_recv()
        for which in (1, 0):
            half = branch if which == 0 else 1 - branch
            lanes = pl.ds(which * features, features)
            summed = None
            for slot in range(heads):
                term = jnp.dot(
                    att[slot, rows, :], w_all[slot, :, lanes], preferred_element_type=F32
                )
                summed = term if summed is None else summed + term
            both = gate[branch, :, gate_cols].astype(F32)
            scale = jnp.where(half == 0, both[0:1], both[1:2])
            hidden = res[half, rows, :].astype(F32) + scale * summed
            if which == 1:
                x_send[rows, :] = hidden.astype(BF)
                exchange(tile).start()
            else:
                own_half[rows, :] = hidden

    def combine(tile):
        exchange(tile).wait_recv()
        frames = TILE // FRAME
        for frame in range(frames):
            rows = pl.ds(tile * TILE + frame * FRAME, FRAME)
            step = guidance[tile * frames + frame].astype(F32)
            strength = 1.0 + 0.5 * step
            mine = jnp.where(branch == 0, strength, 1.0 - strength)
            theirs = 1.0 - mine
            guided = own_half[rows, :] * mine + x_recv[rows, :].astype(F32) * theirs
            out_v[rows, :] = guided.astype(BF)
        rows = pl.ds(tile * TILE, TILE)
        pltpu.make_async_copy(out_v.at[rows], out_hbm.at[rows], out_sem.at[tile]).start()

    for copy in near_copies:
        copy.wait_recv()

    @pl.loop(0, PIECES)
    def _(index):
        begun = jnp.where(index == 0, 0, pick(index - 1, BEGUN))

        @pl.loop(begun, pick(index, BEGUN))
        def _(ahead):
            begin_unit(ahead)

        had = jnp.where(index == 0, 0, pick(index - 1, NEEDED))
        need = pick(index, NEEDED)
        for more in range(2):

            @pl.when(had + more < need)
            def _():
                take_piece(had + more)

        @pl.when(index == SHARE_AT)
        def _():
            share_weights()

        tile, own_head = pick(index, UNIT_ORDER, 0), pick(index, UNIT_ORDER, 1)
        end_unit(tile, own_head, index)
        for kind in (0, 1):
            gather_copy(tile, own_head, kind).start()
        direct = False
        for i in DIRECT:
            direct = jnp.logical_or(direct, index == i)

        @pl.when(direct)
        def _():
            gather_copy(tile, own_head, 4).start()

        behind = index - LAG
        relayed = behind >= 0
        for i in DIRECT:
            relayed = jnp.logical_and(relayed, behind != i)

        @pl.when(relayed)
        def _():
            relay(pick(behind, UNIT_ORDER, 0), pick(behind, UNIT_ORDER, 1))

        @pl.when(index == PROJECT_AT)
        def _():
            for slot in range(1, heads):
                w_share(slot, others).wait_recv()
            project(0)

    for index in range(PIECES - LAG, PIECES):
        if index not in DIRECT:
            relay(*UNIT_ORDER[index])
    for tile in range(1, tiles):
        project(tile)
    for tile in range(tiles):
        combine(tile)

    for tile in range(tiles):
        rows = pl.ds(tile * TILE, TILE)
        pltpu.make_async_copy(out_v.at[rows], out_hbm.at[rows], out_sem.at[tile]).wait()
        exchange(tile).wait_send()
    for d in range(1, heads):
        w_share(d, mine).wait_send()
        for copy in w_copies(d):
            copy.wait_send()

    @pl.loop(0, PIECES)
    def _(index):
        tile, own_head = pick(index, UNIT_ORDER, 0), pick(index, UNIT_ORDER, 1)
        for kind in (0, 1):
            gather_copy(tile, own_head, kind).wait_send()
        direct = False
        for i in DIRECT:
            direct = jnp.logical_or(direct, index == i)

        @pl.when(direct)
        def _():
            gather_copy(tile, own_head, 4).wait_send()

        @pl.when(jnp.logical_not(direct))
        def _():
            for kind in (2, 3):
                gather_copy(tile, own_head, kind).wait_send()

        @pl.when(has_far)
        def _():
            for copy in far_copies(index):
                copy.wait_send()

    for copy in near_copies:
        copy.wait_send()


def local(queries, keys, values, residual, gate, out_weight, time_offsets, guidance_index):
    rows, features = queries.shape[1:]
    heads = lax.axis_size("head")
    smem = pl.BlockSpec(memory_space=pltpu.SMEM)
    vmem = pl.BlockSpec(memory_space=pltpu.VMEM)
    hbm = pl.BlockSpec(memory_space=pl.ANY)
    block = pltpu.VMEM((rows, features), BF)
    dma = pltpu.SemaphoreType.DMA
    tiles = rows // TILE
    return pl.pallas_call(
        kernel,
        out_shape=jax.ShapeDtypeStruct((rows, features), BF),
        in_specs=[smem, smem, vmem, hbm, hbm, hbm, hbm, hbm],
        out_specs=hbm,
        scratch_shapes=[block] * 7
        + [
            pltpu.VMEM((rows, 2, features), BF),
            pltpu.VMEM((2, rows, features), BF),
            pltpu.VMEM((heads, features, 2 * features), BF),
            pltpu.VMEM((heads, rows, features), BF),
            pltpu.VMEM((TILE, 4 * TILE), F32),
            pltpu.VMEM((PIECES, TILE, HD), F32),
            pltpu.VMEM((PIECES, TILE, 2 * HD), F32),
            pltpu.VMEM((rows, features), F32),
            block,
            block,
            block,
            dma((6,)),
            dma((2,)),
            dma((2,)),
            dma((PIECES, 2)),
            dma((PIECES, 2)),
            dma((heads - 1, 2)),
            dma((heads - 1, 2)),
            dma((heads - 1,)),
            dma((heads - 1,)),
            dma((PIECES, 5)),
            dma((PIECES, 5)),
            dma((tiles,)),
            dma((tiles,)),
            dma((tiles,)),
        ],
        compiler_params=pltpu.CompilerParams(
            collective_id=0, has_side_effects=True, vmem_limit_bytes=VMEM
        ),
        name="block",
    )(time_offsets, guidance_index, gate, queries[0], keys[0], values[0], residual[0], out_weight)


def solution(mesh):
    return jax.shard_map(
        local,
        mesh=mesh,
        in_specs=(
            P("branch", "tokens", "head"),
            P("branch", "tokens", "head"),
            P("branch", "tokens", "head"),
            P("branch", "tokens", None, "head"),
            P(),
            P("head", None),
            P(),
            P(),
        ),
        out_specs=P("tokens", ("branch", "head")),
        check_vma=False,
    )
```

time: 89.8 us -> 77.9 us (0.87)
  the two profiles are of different devices: /device:TPU:1 before, /device:TPU:129 now
where the time goes in v2:
time: 77.9 us; the launch traced here: 77.6 us
  Pallas kernels  75.4 us (97%)
  local copies, waits for them, and re-layouts  2.17 us (3%)
    pallas_call x1, Pallas kernels, local(): pl.pallas_call(kernel, out_shape=jax.ShapeDtypeStruct((rows, features), B...  75.4 us
    unnamed x1, local copies, waits for them, and re-layouts  2.17 us

profile of v2, /device:TPU:129, one launch (start us, length us, event | category | flops | bytes accessed | tf_op | source)
XLA Modules:
  0.0 77.6 jit_solution(1649643675569574046)
XLA Ops:
  0.0 75.4 %block.1 = bf16[1152,384]{1,0:T(8,128)(2,1)} custom-call(s32[3,32]{1,0:T(4,128)} %offsets.1, s32[18]{0:T(128)} %guidance.1, bf16[2,2,1536]{2,1,0:T(2,128)(2,1)} %gate.1, bf16[1152,384]{1,0:T(8,128)(2,1)} %bitcast.5, bf16[1152,384]{1,0:T(8,128)(2,1)} %bitcast.6, bf16[1152,384]{1,0:T(8,128)(2,1)} %bitcast.7, bf16[1152,2,384]{2,1,0:T(2,128)(2,1)} %bitcast.4, ...), custom_call_target="tpu_custom_call" | custom-call | tf_op jit(solution)/shard_map/block/pallas_call | solution.py:441
  75.4 2.2 %copy.10 = bf16[1152,384]{1,0:T(8,128)(2,1)} copy(bf16[1152,384]{1,0:T(8,128)(2,1)} %block.1) | data formatting | bytes 1769472

commit v3 on v2

--- a/solution.py
+++ b/solution.py
@@ -13,15 +13,28 @@
 BF = jnp.bfloat16
 F32 = jnp.float32
 SCALE = math.log2(math.e) / math.sqrt(HD)
-WINDOW = 3
+WINDOWS = (4, 2)
 PIECES = 9
 VMEM = 62 * 2**20
 PIECE_ORDER = ((0, 0), (1, 0), (2, 0), (0, 1), (1, 1), (0, 2), (1, 2), (2, 1), (2, 2))
 UNIT_ORDER = ((0, 0), (1, 0), (2, 0), (0, 1), (0, 2), (1, 1), (2, 1), (1, 2), (2, 2))
-NEEDED = (2, 3, 3, 5, 7, 8, 8, 9, 9)
-BEGUN = (2, 3, 3, 6, 9, 9, 9, 9, 9)
-DIRECT = (4, 7, 8)
-LAG = 2
+STEPS = (
+    (0, None, None, None),
+    (1, 0, None, None),
+    (2, 1, 0, None),
+    (3, 2, 1, None),
+    (None, None, 2, None),
+    (4, 3, None, 0),
+    (5, 4, 3, 1),
+    (6, 5, None, 2),
+    (7, 6, 4, 3),
+    (8, 7, 5, None),
+    (None, None, 6, None),
+    (None, 8, 7, None),
+    (None, None, 8, None),
+)
+DIRECT = (4, 5, 7)
+HELD = (6, 8)
 SHARE_AT = 2
 PROJECT_AT = 6
 
@@ -36,9 +49,9 @@
 
 
 def kernel(
-    offsets, guidance, gate, q_hbm, k_hbm, v_hbm, r_hbm, w_hbm, out_hbm,
+    offsets, guidance, gate, q_hbm, k_hbm, v_hbm, r_hbm, w_hbm, own_hbm, came_hbm,
     q_own, k_own, v_own, k_near, v_near, k_far, v_far, res_raw, res, w_all, att, scores, tops, totals,
-    own_half, x_send, x_recv, out_v,
+    own_half, x_send,
     local_sem, near_send, near_recv, halo_send, halo_recv, w_send, w_recv, s_send, s_recv, a_send, a_recv, x_ssem, x_rsem, out_sem,
 ):
     branch = lax.axis_index("branch")
@@ -55,6 +68,8 @@
     sibling = width + step
     far = width - step
     has_far = jnp.logical_and(far >= 0, far < widths)
+    same_z = lax.rem(width + 1, 4) >= 2
+    window = jnp.where(same_z, WINDOWS[0], WINDOWS[1])
     peers = [lax.rem(head + d, heads) for d in range(1, heads)]
 
     def mine_columns(which, owner):
@@ -132,12 +147,16 @@
             for copy in far_copies(index):
                 copy.wait_recv()
 
-        @pl.when(index + WINDOW < PIECES)
-        def _():
-            send_piece(index + WINDOW)
-
-    for index in range(WINDOW):
-        send_piece(index)
+        @pl.when(index + window < PIECES)
+        def _():
+            send_piece(index + window)
+
+    for index in range(max(WINDOWS)):
+
+        @pl.when(index < window)
+        def _():
+            send_piece(index)
+
 
     share = features // 2
     mine = pl.ds(pl.multiple_of(lax.rem(width, 2) * share, share), share)
@@ -289,12 +308,17 @@
         rows = pl.ds(tile * TILE, TILE)
         return pltpu.make_async_remote_copy(
             src_ref=x_send.at[rows],
-            dst_ref=x_recv.at[rows],
+            dst_ref=came_hbm.at[rows],
             send_sem=x_ssem.at[tile],
             recv_sem=x_rsem.at[tile],
             device_id={"branch": 1 - branch},
         )
 
+    def own_copy(tile):
+        rows = pl.ds(tile * TILE, TILE)
+        return pltpu.make_async_copy(own_half.at[rows], own_hbm.at[rows], out_sem.at[tile])
+
+    frames = TILE // FRAME
     gate_cols = pl.ds(pl.multiple_of(head * features, HD), features)
 
     def project(tile):
@@ -315,53 +339,39 @@
             both = gate[branch, :, gate_cols].astype(F32)
             scale = jnp.where(half == 0, both[0:1], both[1:2])
             hidden = res[half, rows, :].astype(F32) + scale * summed
+            for frame in range(frames):
+                part = pl.ds(tile * TILE + frame * FRAME, FRAME)
+                strength = 1.0 + 0.5 * guidance[tile * frames + frame].astype(F32)
+                mine = jnp.where(branch == 0, strength, 1.0 - strength)
+                scaled = hidden[frame * FRAME : (frame + 1) * FRAME] * mine
+                if which == 1:
+                    x_send[part, :] = scaled.astype(BF)
+                else:
+                    own_half[part, :] = scaled
             if which == 1:
-                x_send[rows, :] = hidden.astype(BF)
                 exchange(tile).start()
             else:
-                own_half[rows, :] = hidden
-
-    def combine(tile):
-        exchange(tile).wait_recv()
-        frames = TILE // FRAME
-        for frame in range(frames):
-            rows = pl.ds(tile * TILE + frame * FRAME, FRAME)
-            step = guidance[tile * frames + frame].astype(F32)
-            strength = 1.0 + 0.5 * step
-            mine = jnp.where(branch == 0, strength, 1.0 - strength)
-            theirs = 1.0 - mine
-            guided = own_half[rows, :] * mine + x_recv[rows, :].astype(F32) * theirs
-            out_v[rows, :] = guided.astype(BF)
-        rows = pl.ds(tile * TILE, TILE)
-        pltpu.make_async_copy(out_v.at[rows], out_hbm.at[rows], out_sem.at[tile]).start()
+                own_copy(tile).start()
 
     for copy in near_copies:
         copy.wait_recv()
 
-    @pl.loop(0, PIECES)
-    def _(index):
-        begun = jnp.where(index == 0, 0, pick(index - 1, BEGUN))
-
-        @pl.loop(begun, pick(index, BEGUN))
-        def _(ahead):
-            begin_unit(ahead)
-
-        had = jnp.where(index == 0, 0, pick(index - 1, NEEDED))
-        need = pick(index, NEEDED)
-        for more in range(2):
-
-            @pl.when(had + more < need)
-            def _():
-                take_piece(had + more)
-
+    def finish(index):
         @pl.when(index == SHARE_AT)
         def _():
             share_weights()
 
         tile, own_head = pick(index, UNIT_ORDER, 0), pick(index, UNIT_ORDER, 1)
         end_unit(tile, own_head, index)
-        for kind in (0, 1):
-            gather_copy(tile, own_head, kind).start()
+        held = False
+        for i in HELD:
+            held = jnp.logical_or(held, index == i)
+
+        @pl.when(jnp.logical_not(held))
+        def _():
+            for kind in (0, 1):
+                gather_copy(tile, own_head, kind).start()
+
         direct = False
         for i in DIRECT:
             direct = jnp.logical_or(direct, index == i)
@@ -370,33 +380,47 @@
         def _():
             gather_copy(tile, own_head, 4).start()
 
-        behind = index - LAG
-        relayed = behind >= 0
-        for i in DIRECT:
-            relayed = jnp.logical_and(relayed, behind != i)
-
-        @pl.when(relayed)
-        def _():
-            relay(pick(behind, UNIT_ORDER, 0), pick(behind, UNIT_ORDER, 1))
-
         @pl.when(index == PROJECT_AT)
         def _():
             for slot in range(1, heads):
                 w_share(slot, others).wait_recv()
             project(0)
 
-    for index in range(PIECES - LAG, PIECES):
-        if index not in DIRECT:
-            relay(*UNIT_ORDER[index])
-    for tile in range(1, tiles):
-        project(tile)
+    @pl.loop(0, len(STEPS))
+    def _(step):
+        begun, taken, ended, relayed = (
+            pick(step, [0 if entry[i] is None else entry[i] + 1 for entry in STEPS])
+            for i in range(4)
+        )
+
+        @pl.when(begun > 0)
+        def _():
+            begin_unit(begun - 1)
+
+        @pl.when(taken > 0)
+        def _():
+            take_piece(taken - 1)
+
+        @pl.when(ended > 0)
+        def _():
+            finish(ended - 1)
+
+        @pl.when(relayed > 0)
+        def _():
+            relay(pick(relayed - 1, UNIT_ORDER, 0), pick(relayed - 1, UNIT_ORDER, 1))
+
+    for kind in (0, 1, 4):
+        gather_copy(*UNIT_ORDER[7], kind).wait_send()
+    for index in HELD:
+        for kind in (0, 1):
+            gather_copy(*UNIT_ORDER[index], kind).start()
+    project(1)
+    for index in HELD:
+        relay(*UNIT_ORDER[index])
+    project(2)
     for tile in range(tiles):
-        combine(tile)
-
-    for tile in range(tiles):
-        rows = pl.ds(tile * TILE, TILE)
-        pltpu.make_async_copy(out_v.at[rows], out_hbm.at[rows], out_sem.at[tile]).wait()
-        exchange(tile).wait_send()
+        own_copy(tile).wait()
+        exchange(tile).wait()
     for d in range(1, heads):
         w_share(d, mine).wait_send()
         for copy in w_copies(d):
@@ -405,13 +429,17 @@
     @pl.loop(0, PIECES)
     def _(index):
         tile, own_head = pick(index, UNIT_ORDER, 0), pick(index, UNIT_ORDER, 1)
-        for kind in (0, 1):
-            gather_copy(tile, own_head, kind).wait_send()
+
+        @pl.when(index != 7)
+        def _():
+            for kind in (0, 1):
+                gather_copy(tile, own_head, kind).wait_send()
+
         direct = False
         for i in DIRECT:
             direct = jnp.logical_or(direct, index == i)
 
-        @pl.when(direct)
+        @pl.when(jnp.logical_and(direct, index != 7))
         def _():
             gather_copy(tile, own_head, 4).wait_send()
 
@@ -434,15 +462,18 @@
     heads = lax.axis_size("head")
     smem = pl.BlockSpec(memory_space=pltpu.SMEM)
     vmem = pl.BlockSpec(memory_space=pltpu.VMEM)
-    hbm = pl.BlockSpec(memory_space=pl.ANY)
+    hbm = pl.BlockSpec(memory_space=pltpu.HBM)
     block = pltpu.VMEM((rows, features), BF)
     dma = pltpu.SemaphoreType.DMA
     tiles = rows // TILE
-    return pl.pallas_call(
+    own, came = pl.pallas_call(
         kernel,
-        out_shape=jax.ShapeDtypeStruct((rows, features), BF),
+        out_shape=[
+            jax.ShapeDtypeStruct((rows, features), F32),
+            jax.ShapeDtypeStruct((rows, features), BF),
+        ],
         in_specs=[smem, smem, vmem, hbm, hbm, hbm, hbm, hbm],
-        out_specs=hbm,
+        out_specs=[pl.BlockSpec(memory_space=pl.ANY)] * 2,
         scratch_shapes=[block] * 7
         + [
             pltpu.VMEM((rows, 2, features), BF),
@@ -453,8 +484,6 @@
             pltpu.VMEM((PIECES, TILE, HD), F32),
             pltpu.VMEM((PIECES, TILE, 2 * HD), F32),
             pltpu.VMEM((rows, features), F32),
-            block,
-            block,
             block,
             dma((6,)),
             dma((2,)),
@@ -476,6 +505,7 @@
         ),
         name="block",
     )(time_offsets, guidance_index, gate, queries[0], keys[0], values[0], residual[0], out_weight)
+    return (own + came.astype(F32)).astype(BF)
 
 
 def solution(mesh):

time: 77.9 us -> 76.6 us (0.983)
  other arithmetic: 0 us -> 2.79 us
  local copies, waits for them, and re-layouts: 2.17 us -> 0 us
  Pallas kernels: 75.4 us -> 73.7 us
    convert_element_type x0 -> x1, other arithmetic: none -> 2.79 us  [local(): return (own + came.astype(F32)).astype(BF)]
    unnamed x1 -> x0, local copies, waits for them, and re-layouts: 2.17 us -> none
    pallas_call x1, Pallas kernels: 75.4 us -> 73.7 us  [local(): pl.pallas_call(kernel, out_shape=[jax.ShapeDtypeStruct((rows, features),...]
where the time goes in v3:
time: 76.6 us; the launch traced here: 76.5 us
  Pallas kernels  73.7 us (96%)
  other arithmetic  2.79 us (4%)
    pallas_call x1, Pallas kernels, local(): pl.pallas_call(kernel, out_shape=[jax.ShapeDtypeStruct((rows, features),...  73.7 us
    convert_element_type x1, other arithmetic, local(): return (own + came.astype(F32)).astype(BF)  2.79 us

profile of v3, /device:TPU:129, one launch (start us, length us, event | category | flops | bytes accessed | tf_op | source)
XLA Modules:
  0.0 76.5 jit_solution(3967375227908059614)
XLA Ops:
  0.0 73.7 %block.1 = (f32[1152,384]{1,0:T(8,128)}, bf16[1152,384]{1,0:T(8,128)(2,1)}) custom-call(s32[3,32]{1,0:T(4,128)} %offsets.1, s32[18]{0:T(128)} %guidance.1, bf16[2,2,1536]{2,1,0:T(2,128)(2,1)} %gate.1, bf16[1152,384]{1,0:T(8,128)(2,1)} %bitcast.5, bf16[1152,384]{1,0:T(8,128)(2,1)} %bitcast.6, bf16[1152,384]{1,0:T(8,128)(2,1)} %bitcast.7, ...), custom_call_target="tpu_custom_call" | custom-call | tf_op jit(solution)/shard_map/block/pallas_call | solution.py:469
  73.7 2.8 %add_convert_fusion = bf16[1152,384]{1,0:T(8,128)(2,1)} fusion(f32[1152,384]{1,0:T(8,128)} %get-tuple-element.7, bf16[1152,384]{1,0:T(8,128)(2,1)} %get-tuple-element.8), kind=kLoop, calls=%fused_computation | loop fusion | flops 1327104 | bytes 3538944 | tf_op jit(solution)/shard_map/convert_element_type | solution.py:508

commit v4 on v3

--- a/solution.py
+++ b/solution.py
@@ -13,7 +13,7 @@
 BF = jnp.bfloat16
 F32 = jnp.float32
 SCALE = math.log2(math.e) / math.sqrt(HD)
-WINDOWS = (4, 2)
+WINDOWS = (5, 3)
 PIECES = 9
 VMEM = 62 * 2**20
 PIECE_ORDER = ((0, 0), (1, 0), (2, 0), (0, 1), (1, 1), (0, 2), (1, 2), (2, 1), (2, 2))
@@ -33,8 +33,8 @@
     (None, 8, 7, None),
     (None, None, 8, None),
 )
-DIRECT = (4, 5, 7)
-HELD = (6, 8)
+DIRECT = (4, 5, 6, 7, 8)
+HELD = ()
 SHARE_AT = 2
 PROJECT_AT = 6
 

time: 76.6 us -> 74 us (0.966)
  Pallas kernels: 73.7 us -> 71 us
    pallas_call x1, Pallas kernels: 73.7 us -> 71 us  [local(): pl.pallas_call(kernel, out_shape=[jax.ShapeDtypeStruct((rows, features),...]
where the time goes in v4:
time: 74 us; the launch traced here: 73.8 us
  Pallas kernels  71 us (96%)
  other arithmetic  2.79 us (4%)
    pallas_call x1, Pallas kernels, local(): pl.pallas_call(kernel, out_shape=[jax.ShapeDtypeStruct((rows, features),...  71 us
    convert_element_type x1, other arithmetic, local(): return (own + came.astype(F32)).astype(BF)  2.79 us

profile of v4, /device:TPU:129, one launch (start us, length us, event | category | flops | bytes accessed | tf_op | source)
XLA Modules:
  0.0 73.8 jit_solution(11460088190448591182)
XLA Ops:
  0.0 71.0 %block.1 = (f32[1152,384]{1,0:T(8,128)}, bf16[1152,384]{1,0:T(8,128)(2,1)}) custom-call(s32[3,32]{1,0:T(4,128)} %offsets.1, s32[18]{0:T(128)} %guidance.1, bf16[2,2,1536]{2,1,0:T(2,128)(2,1)} %gate.1, bf16[1152,384]{1,0:T(8,128)(2,1)} %bitcast.5, bf16[1152,384]{1,0:T(8,128)(2,1)} %bitcast.6, bf16[1152,384]{1,0:T(8,128)(2,1)} %bitcast.7, ...), custom_call_target="tpu_custom_call" | custom-call | tf_op jit(solution)/shard_map/block/pallas_call | solution.py:469
  71.0 2.8 %add_convert_fusion = bf16[1152,384]{1,0:T(8,128)(2,1)} fusion(f32[1152,384]{1,0:T(8,128)} %get-tuple-element.7, bf16[1152,384]{1,0:T(8,128)(2,1)} %get-tuple-element.8), kind=kLoop, calls=%fused_computation | loop fusion | flops 1327104 | bytes 3538944 | tf_op jit(solution)/shard_map/convert_element_type | solution.py:508
